TPU v7x, 32 devices: a whole 2x2x4 slice. The times are simulated.
32 devices in a mesh: ctx: 8 (over z, x), chan: 4 (over y, core).
Axes of the slice: x: 2, y: 2, z: 4, core: 2. Of those that a mesh axis runs over, the one named last changes fastest.
Arguments:
- signal: bfloat16 [2048, 4096], P('ctx', 'chan'), may hold values from -6 to 6
- gate_values: bfloat16 [2048, 4096], P('ctx', 'chan'), may hold values from -6 to 6
- skip_gain: float32 [4096], P('chan'), may hold values from 0.5 to 1.5
- filter_base: bfloat16 [64, 16384], P('chan', 'ctx'), may hold values from -0.09375 to 0.09375
- decay_rate: float32 [64], P('chan'), may hold values from 0.3 to 30
- filter_depth: int32 [64], P('chan'), may hold values from 2048 to 16384
- doc_starts: int32 [5], replicated, may hold values from 0 to 512, as said below
Outputs:
- mixed: bfloat16 [2048, 4096], P('ctx', 'chan')
Inputs may be any that keep to these rules, and one draw needn't show every extreme that they name: doc_starts[0] is 0 and the starts rise strictly; document k runs from doc_starts[k] up to the position before the next start, the last one to the end of the window.
All inputs are finite; a program needn't handle non-finite values.
Results may differ from a plain program's by a relative error of at most 0.0026.
Values may be sent and summed in bfloat16 or wider, within the bound.
A program may use at most 64 MiB of HBM per device.

v0:
```python
import jax
import jax.numpy as jnp
from jax import lax
from jax.sharding import PartitionSpec as P

LAGS = 16384


def begin_rows(doc_starts, positions):
    return jnp.max(
        jnp.where(doc_starts[None, :] <= positions[:, None], doc_starts[None, :], 0), axis=1
    )


def toeplitz_apply(summed, padded, margin, lag_total, out_first, doc_begin, source, anchor):
    out_rows, chan_width = summed.shape
    group_count = padded.shape[0]
    group_size = chan_width // group_count
    source_rows = source.shape[0]
    window_size = out_rows + source_rows - 1
    lowest = out_first - anchor - source_rows + 1
    offset = jnp.clip(lowest, -window_size, lag_total) + margin
    window = lax.dynamic_slice_in_dim(padded, offset, window_size, 1)
    extended = jnp.pad(window, ((0, 0), (0, 1)))
    repeated = jnp.tile(extended, (1, out_rows + 1))
    skewed = repeated[:, : out_rows * (window_size + 2)].reshape(
        group_count, out_rows, window_size + 2
    )
    toeplitz = skewed[:, :, :source_rows][:, :, ::-1]
    doc_mask = (anchor + lax.iota(jnp.int32, source_rows))[None, :] >= doc_begin[:, None]
    toeplitz = jnp.where(doc_mask[None], toeplitz, jnp.zeros((), jnp.bfloat16))
    channels = source.reshape(source_rows, group_count, group_size)
    product = jnp.einsum("gts,sgc->tgc", toeplitz, channels, preferred_element_type=jnp.float32)
    return summed + product.reshape(out_rows, chan_width)


def body(signal, gate_values, skip_gain, filter_base, decay_rate, filter_depth, doc_starts):
    tok_rows, chan_width = signal.shape
    group_count, lag_width = filter_base.shape
    ctx_index = lax.axis_index("ctx")
    lag_index = ctx_index * lag_width + lax.iota(jnp.int32, lag_width)
    inside = lag_index[None, :] < filter_depth[:, None]
    local_panel = jnp.where(
        inside,
        filter_base.astype(jnp.float32)
        * jnp.exp(-decay_rate[:, None] * lag_index.astype(jnp.float32)[None, :] / LAGS),
        0.0,
    ).astype(jnp.bfloat16)
    filters = lax.all_gather(local_panel, "ctx", axis=1, tiled=True)
    lag_total = filters.shape[1]
    margin = 2 * tok_rows
    padded = jnp.pad(filters, ((0, 0), (margin, margin)))
    first_row = ctx_index * tok_rows
    positions = first_row + lax.iota(jnp.int32, tok_rows)
    doc_begin = begin_rows(doc_starts, positions)

    def add_checked(summed, source, anchor):
        needed = anchor < first_row + tok_rows
        return lax.cond(
            needed,
            lambda carried: toeplitz_apply(
                carried, padded, margin, lag_total, first_row, doc_begin, source, anchor
            ),
            lambda carried: carried,
            summed,
        )

    initial = jnp.zeros((tok_rows, chan_width), jnp.float32)
    summed = initial
    source = lax.all_gather(signal, "ctx", axis=0, tiled=True)
    source_rows = source.shape[0]
    steps_count = source_rows // tok_rows
    stacked = source.reshape(steps_count, tok_rows, chan_width)

    def advance(carried, item):
        one_shard, number = item
        return (add_checked(carried, one_shard, number * tok_rows), None)

    summed, ignored = lax.scan(advance, summed, (stacked, jnp.arange(steps_count, dtype=jnp.int32)))
    mixed = gate_values.astype(jnp.float32) * (
        summed + skip_gain[None, :] * signal.astype(jnp.float32)
    )
    return mixed.astype(jnp.bfloat16)


def solution(mesh):
    in_specs = (
        P("ctx", "chan"),
        P("ctx", "chan"),
        P("chan"),
        P("chan", "ctx"),
        P("chan"),
        P("chan"),
        P(),
    )
    out_specs = P("ctx", "chan")
    return jax.shard_map(body, mesh=mesh, in_specs=in_specs, out_specs=out_specs, check_vma=False)
```

profile of v0, /device:TPU:26, one launch (start us, length us, event | category | flops | bytes accessed | tf_op | source)
XLA Modules:
  0.0 476.9 jit_solution(17988195457726684929)
XLA Ops:
  8.9 32.5 %all_gather.6 = bf16[16,16384]{1,0:T(8,128)(2,1)S(1)} all-gather(bf16[16,2048]{1,0:T(8,128)(2,1)S(1)} %select_convert_fusion), channel_id=1, replica_groups=mesh['ctx'=8,'chan'=4] {'ctx'}, dimensions={1}, use_global_device_ids=true | all-gather | bytes 589824 | tf_op jit(solution)/shard_map/all_gather | solution.py:49
  43.0 41.0 %all-gather.2.cloned.1.call-done = bf16[2048,1024]{1,0:T(8,128)(2,1)} async-done(((bf16[256,1024]{1,0:T(8,128)(2,1)}), bf16[2048,1024]{1,0:T(8,128)(2,1)}) %all-gather.2.cloned.1.call-update) | async-done | bytes 4194320 | tf_op jit(solution)/shard_map/all_gather | solution.py:70
  84.0 6.4 %copy.11 = bf16[8,256,1024]{1,2,0:T(8,128)(2,1)} copy(bf16[8,256,1024]{2,1,0:T(8,128)(2,1)} %bitcast.15) | data formatting | bytes 8388608 | tf_op jit(solution)/shard_map/while | solution.py:79
  90.5 376.9 %while.14 = (s32[]{:T(128)}, f32[256,1024]{0,1:T(8,128)S(1)}, s32[8]{0:T(128)S(1)}, s32[]{:T(128)}, s32[256]{0:T(256)S(1)}, /*index=5*/s32[]{:T(128)}, bf16[16,1...) while((s32[]{:T(128)}, f32[256,1024]{0,1:T(8,128)S(1)}, s32[8]{0:T(128)S(1)}, ...), condition=%wide.region_4.5_spmd, body=%wide.region_1.4_spmd.sunk | while | flops 135594240 | bytes 48008432 | solution.py:79
  91.7 45.9 %conditional.2 = (f32[256,1024]{0,1:T(8,128)S(1)}) conditional(s32[]{:T(128)} %convert_element_type.43, f32[256,1024]{0,1:T(8,128)S(1)} %get-tuple-element.213, (s32[]{:T(128)}, s32[256]{0:T(256)S(1)}, s32[]{:T(128)}, bf16[16,17408]{1,0:T(8,128)(2,1)}, bf16[8,256,1024]{1,2,0:T(8,128)(2,1)}, /*index=5*/s32[]{:T(128)}, f32[256,1024]{0,1:T(8,128)S(1)}) %tuple.36), branch_computations={%region_2.2_spmd, %region_3.3_spmd} | conditional | flops 135594240 | bytes 48008236 | solution.py:59
  96.6 13.3 %reshape.66 = bf16[16,256,513]{2,1,0:T(8,128)(2,1)} reshape(bf16[16,131328]{1,0:T(8,128)(2,1)} %slice.8) | data formatting | bytes 8404992 | tf_op jit(solution)/shard_map/while/body/eval_jaxpr/cond/branch_1_fun/reshape | solution.py:26
  111.5 22.4 %rev.3 = bf16[16,256,256]{2,1,0:T(8,128)(2,1)} reverse(bf16[16,256,256]{2,1,0:T(8,128)(2,1)S(1)} %slice-done), dimensions={2} | reverse | bytes 4194304 | tf_op jit(solution)/shard_map/while/body/eval_jaxpr/cond/branch_1_fun/rev | solution.py:29
  138.9 45.9 %conditional.2 = (f32[256,1024]{0,1:T(8,128)S(1)}) conditional(s32[]{:T(128)} %convert_element_type.43, f32[256,1024]{0,1:T(8,128)S(1)} %get-tuple-element.213, (s32[]{:T(128)}, s32[256]{0:T(256)S(1)}, s32[]{:T(128)}, bf16[16,17408]{1,0:T(8,128)(2,1)}, bf16[8,256,1024]{1,2,0:T(8,128)(2,1)}, /*index=5*/s32[]{:T(128)}, f32[256,1024]{0,1:T(8,128)S(1)}) %tuple.36), branch_computations={%region_2.2_spmd, %region_3.3_spmd} | conditional | flops 135594240 | bytes 48008236 | solution.py:59
  143.7 13.3 %reshape.66 = bf16[16,256,513]{2,1,0:T(8,128)(2,1)} reshape(bf16[16,131328]{1,0:T(8,128)(2,1)} %slice.8) | data formatting | bytes 8404992 | tf_op jit(solution)/shard_map/while/body/eval_jaxpr/cond/branch_1_fun/reshape | solution.py:26
  158.6 22.4 %rev.3 = bf16[16,256,256]{2,1,0:T(8,128)(2,1)} reverse(bf16[16,256,256]{2,1,0:T(8,128)(2,1)S(1)} %slice-done), dimensions={2} | reverse | bytes 4194304 | tf_op jit(solution)/shard_map/while/body/eval_jaxpr/cond/branch_1_fun/rev | solution.py:29
  182.2 2.4 fusion
  186.0 45.9 %conditional.2 = (f32[256,1024]{0,1:T(8,128)S(1)}) conditional(s32[]{:T(128)} %convert_element_type.43, f32[256,1024]{0,1:T(8,128)S(1)} %get-tuple-element.213, (s32[]{:T(128)}, s32[256]{0:T(256)S(1)}, s32[]{:T(128)}, bf16[16,17408]{1,0:T(8,128)(2,1)}, bf16[8,256,1024]{1,2,0:T(8,128)(2,1)}, /*index=5*/s32[]{:T(128)}, f32[256,1024]{0,1:T(8,128)S(1)}) %tuple.36), branch_computations={%region_2.2_spmd, %region_3.3_spmd} | conditional | flops 135594240 | bytes 48008236 | solution.py:59
  190.8 13.3 %reshape.66 = bf16[16,256,513]{2,1,0:T(8,128)(2,1)} reshape(bf16[16,131328]{1,0:T(8,128)(2,1)} %slice.8) | data formatting | bytes 8404992 | tf_op jit(solution)/shard_map/while/body/eval_jaxpr/cond/branch_1_fun/reshape | solution.py:26
  205.7 22.4 %rev.3 = bf16[16,256,256]{2,1,0:T(8,128)(2,1)} reverse(bf16[16,256,256]{2,1,0:T(8,128)(2,1)S(1)} %slice-done), dimensions={2} | reverse | bytes 4194304 | tf_op jit(solution)/shard_map/while/body/eval_jaxpr/cond/branch_1_fun/rev | solution.py:29
  233.1 45.9 %conditional.2 = (f32[256,1024]{0,1:T(8,128)S(1)}) conditional(s32[]{:T(128)} %convert_element_type.43, f32[256,1024]{0,1:T(8,128)S(1)} %get-tuple-element.213, (s32[]{:T(128)}, s32[256]{0:T(256)S(1)}, s32[]{:T(128)}, bf16[16,17408]{1,0:T(8,128)(2,1)}, bf16[8,256,1024]{1,2,0:T(8,128)(2,1)}, /*index=5*/s32[]{:T(128)}, f32[256,1024]{0,1:T(8,128)S(1)}) %tuple.36), branch_computations={%region_2.2_spmd, %region_3.3_spmd} | conditional | flops 135594240 | bytes 48008236 | solution.py:59
  237.9 13.3 %reshape.66 = bf16[16,256,513]{2,1,0:T(8,128)(2,1)} reshape(bf16[16,131328]{1,0:T(8,128)(2,1)} %slice.8) | data formatting | bytes 8404992 | tf_op jit(solution)/shard_map/while/body/eval_jaxpr/cond/branch_1_fun/reshape | solution.py:26
  252.8 22.4 %rev.3 = bf16[16,256,256]{2,1,0:T(8,128)(2,1)} reverse(bf16[16,256,256]{2,1,0:T(8,128)(2,1)S(1)} %slice-done), dimensions={2} | reverse | bytes 4194304 | tf_op jit(solution)/shard_map/while/body/eval_jaxpr/cond/branch_1_fun/rev | solution.py:29
  276.4 2.4 fusion
  280.2 45.9 %conditional.2 = (f32[256,1024]{0,1:T(8,128)S(1)}) conditional(s32[]{:T(128)} %convert_element_type.43, f32[256,1024]{0,1:T(8,128)S(1)} %get-tuple-element.213, (s32[]{:T(128)}, s32[256]{0:T(256)S(1)}, s32[]{:T(128)}, bf16[16,17408]{1,0:T(8,128)(2,1)}, bf16[8,256,1024]{1,2,0:T(8,128)(2,1)}, /*index=5*/s32[]{:T(128)}, f32[256,1024]{0,1:T(8,128)S(1)}) %tuple.36), branch_computations={%region_2.2_spmd, %region_3.3_spmd} | conditional | flops 135594240 | bytes 48008236 | solution.py:59
  285.1 13.3 %reshape.66 = bf16[16,256,513]{2,1,0:T(8,128)(2,1)} reshape(bf16[16,131328]{1,0:T(8,128)(2,1)} %slice.8) | data formatting | bytes 8404992 | tf_op jit(solution)/shard_map/while/body/eval_jaxpr/cond/branch_1_fun/reshape | solution.py:26
  300.0 22.4 %rev.3 = bf16[16,256,256]{2,1,0:T(8,128)(2,1)} reverse(bf16[16,256,256]{2,1,0:T(8,128)(2,1)S(1)} %slice-done), dimensions={2} | reverse | bytes 4194304 | tf_op jit(solution)/shard_map/while/body/eval_jaxpr/cond/branch_1_fun/rev | solution.py:29
  327.3 45.9 %conditional.2 = (f32[256,1024]{0,1:T(8,128)S(1)}) conditional(s32[]{:T(128)} %convert_element_type.43, f32[256,1024]{0,1:T(8,128)S(1)} %get-tuple-element.213, (s32[]{:T(128)}, s32[256]{0:T(256)S(1)}, s32[]{:T(128)}, bf16[16,17408]{1,0:T(8,128)(2,1)}, bf16[8,256,1024]{1,2,0:T(8,128)(2,1)}, /*index=5*/s32[]{:T(128)}, f32[256,1024]{0,1:T(8,128)S(1)}) %tuple.36), branch_computations={%region_2.2_spmd, %region_3.3_spmd} | conditional | flops 135594240 | bytes 48008236 | solution.py:59
  332.2 13.3 %reshape.66 = bf16[16,256,513]{2,1,0:T(8,128)(2,1)} reshape(bf16[16,131328]{1,0:T(8,128)(2,1)} %slice.8) | data formatting | bytes 8404992 | tf_op jit(solution)/shard_map/while/body/eval_jaxpr/cond/branch_1_fun/reshape | solution.py:26
  347.1 22.4 %rev.3 = bf16[16,256,256]{2,1,0:T(8,128)(2,1)} reverse(bf16[16,256,256]{2,1,0:T(8,128)(2,1)S(1)} %slice-done), dimensions={2} | reverse | bytes 4194304 | tf_op jit(solution)/shard_map/while/body/eval_jaxpr/cond/branch_1_fun/rev | solution.py:29
  370.7 2.4 fusion
  374.4 45.9 %conditional.2 = (f32[256,1024]{0,1:T(8,128)S(1)}) conditional(s32[]{:T(128)} %convert_element_type.43, f32[256,1024]{0,1:T(8,128)S(1)} %get-tuple-element.213, (s32[]{:T(128)}, s32[256]{0:T(256)S(1)}, s32[]{:T(128)}, bf16[16,17408]{1,0:T(8,128)(2,1)}, bf16[8,256,1024]{1,2,0:T(8,128)(2,1)}, /*index=5*/s32[]{:T(128)}, f32[256,1024]{0,1:T(8,128)S(1)}) %tuple.36), branch_computations={%region_2.2_spmd, %region_3.3_spmd} | conditional | flops 135594240 | bytes 48008236 | solution.py:59
  379.3 13.3 %reshape.66 = bf16[16,256,513]{2,1,0:T(8,128)(2,1)} reshape(bf16[16,131328]{1,0:T(8,128)(2,1)} %slice.8) | data formatting | bytes 8404992 | tf_op jit(solution)/shard_map/while/body/eval_jaxpr/cond/branch_1_fun/reshape | solution.py:26
  394.2 22.4 %rev.3 = bf16[16,256,256]{2,1,0:T(8,128)(2,1)} reverse(bf16[16,256,256]{2,1,0:T(8,128)(2,1)S(1)} %slice-done), dimensions={2} | reverse | bytes 4194304 | tf_op jit(solution)/shard_map/while/body/eval_jaxpr/cond/branch_1_fun/rev | solution.py:29
  421.6 45.9 %conditional.2 = (f32[256,1024]{0,1:T(8,128)S(1)}) conditional(s32[]{:T(128)} %convert_element_type.43, f32[256,1024]{0,1:T(8,128)S(1)} %get-tuple-element.213, (s32[]{:T(128)}, s32[256]{0:T(256)S(1)}, s32[]{:T(128)}, bf16[16,17408]{1,0:T(8,128)(2,1)}, bf16[8,256,1024]{1,2,0:T(8,128)(2,1)}, /*index=5*/s32[]{:T(128)}, f32[256,1024]{0,1:T(8,128)S(1)}) %tuple.36), branch_computations={%region_2.2_spmd, %region_3.3_spmd} | conditional | flops 135594240 | bytes 48008236 | solution.py:59
  426.4 13.3 %reshape.66 = bf16[16,256,513]{2,1,0:T(8,128)(2,1)} reshape(bf16[16,131328]{1,0:T(8,128)(2,1)} %slice.8) | data formatting | bytes 8404992 | tf_op jit(solution)/shard_map/while/body/eval_jaxpr/cond/branch_1_fun/reshape | solution.py:26
  441.3 22.4 %rev.3 = bf16[16,256,256]{2,1,0:T(8,128)(2,1)} reverse(bf16[16,256,256]{2,1,0:T(8,128)(2,1)S(1)} %slice-done), dimensions={2} | reverse | bytes 4194304 | tf_op jit(solution)/shard_map/while/body/eval_jaxpr/cond/branch_1_fun/rev | solution.py:29
  464.9 2.4 fusion
  (114 shorter events, 83.4 us)
Async XLA Ops:
  6.5 77.5 %all-gather.2.cloned.1.call-start = ((), (), s32[]{:S(2)}) async-start(), calls=%async_computation | async-start | bytes 4718592 | tf_op jit(solution)/shard_map/all_gather | solution.py:70
  90.5 377.3 %copy-start = (f32[1024]{0:T(1024)S(1)}, f32[1024]{0:T(1024)}, u32[]{:S(2)}) copy-start(f32[1024]{0:T(1024)} %param.13) | copy-start | bytes 12292
  109.9 1.6 slice-start
  157.0 1.6 slice-start
  204.1 1.6 slice-start
  251.2 1.6 slice-start
  298.4 1.6 slice-start
  345.5 1.6 slice-start
  392.6 1.6 slice-start
  439.7 1.6 slice-start
Sparse Core Ops, SparseCore 0:
  9.5 74.4 all-gather.1
where the time goes:
time: 479 us; the launch traced here: 477 us
  local copies, waits for them, and re-layouts  358 us (75%)
  waiting for transfers between devices  41.7 us (9%)
  blocking collectives  32.5 us (7%)
  matrix products  18.8 us (4%)
  between operations  13.4 us (3%)
  other arithmetic  7.3 us (2%)
  loops' own time  5.29 us (1%)
    rev x8, local copies, waits for them, and re-layouts, toeplitz_apply(): toeplitz = skewed[:, :, :source_rows][:, :, ::-1]  179 us
    reshape x8, local copies, waits for them, and re-layouts, toeplitz_apply(): repeated[:, :out_rows * (window_size + 2)]  106 us
    all_gather x1, waiting for transfers between devices, body(): source = lax.all_gather(signal, 'ctx', axis=0, tiled=True)  41 us
    all_gather x1, blocking collectives, body(): filters = lax.all_gather(local_panel, 'ctx', axis=1, tiled=True)  32.5 us
    dot_general x8, matrix products, toeplitz_apply(): jnp.einsum('gts,sgc->tgc', toeplitz, channels, preferred_element_type=jnp...  18.8 us
    slice x8, local copies, waits for them, and re-layouts, toeplitz_apply(): repeated[:, :out_rows * (window_size + 2)]  17.3 us
    dynamic_slice x16, local copies, waits for them, and re-layouts, body(): lax.scan(advance, summed, (stacked, jnp.arange(steps_count, dtype=jnp.int...  13.4 us
    slice x16, local copies, waits for them, and re-layouts, toeplitz_apply(): toeplitz = skewed[:, :, :source_rows][:, :, ::-1]  12.7 us
  transfers between devices with their start and end apart: 1, of which 1 were waited for; matrix products, arithmetic and copies ran while one was open for 1% of the time, Pallas kernels for 0%

commit v1 on v0

--- a/solution.py
+++ b/solution.py
@@ -1,6 +1,10 @@
+import functools
+
 import jax
 import jax.numpy as jnp
 from jax import lax
+from jax.experimental import pallas as pl
+from jax.experimental.pallas import tpu as pltpu
 from jax.sharding import PartitionSpec as P
 
 LAGS = 16384
@@ -34,7 +38,7 @@
     return summed + product.reshape(out_rows, chan_width)
 
 
-def body(signal, gate_values, skip_gain, filter_base, decay_rate, filter_depth, doc_starts):
+def gathered_body(signal, gate_values, skip_gain, filter_base, decay_rate, filter_depth, doc_starts):
     tok_rows, chan_width = signal.shape
     group_count, lag_width = filter_base.shape
     ctx_index = lax.axis_index("ctx")
@@ -83,6 +87,273 @@
     return mixed.astype(jnp.bfloat16)
 
 
+LINK = jnp.int16
+TOP = 32000.0
+TAIL = 16
+MESH = pl.DeviceIdType.MESH
+
+
+def store_coded(y_buf, block, total):
+    rows, width = total.shape
+    peak = jnp.maximum(jnp.max(jnp.abs(total), axis=0, keepdims=True), 1e-30)
+    exponent = jnp.ceil(jnp.log2(peak))
+    coded = jnp.floor(total * (jnp.exp2(-exponent) * TOP) + 0.5)
+    first = block * (rows + TAIL)
+    y_buf[pl.ds(first, rows), :] = coded.astype(jnp.int32).astype(LINK)
+    tail = jnp.broadcast_to(exponent, (TAIL, width))
+    y_buf[pl.ds(first + rows, TAIL), :] = tail.astype(jnp.int32).astype(LINK)
+
+
+def exchange_kernel(
+    count, masked_blocks, signal_ref, taps_ref, starts_ref, out_ref,
+    taps_buf, x_buf, y_buf, strip, local_sems, taps_send, taps_recv, send_x, recv_x, send_y, recv_y,
+):
+    me = lax.axis_index("ctx")
+    rows = x_buf.shape[0] // count
+    width = x_buf.shape[1]
+    tap_rows = taps_buf.shape[0]
+    groups = tap_rows // count
+    window = rows * count
+
+    def peer_at(offset):
+        return lax.rem(me + offset, count)
+
+    def lanes(index):
+        return pl.ds(pl.multiple_of(index * width, width), width)
+
+    def row_block(index):
+        return pl.ds(pl.multiple_of(index * rows, rows), rows)
+
+    def coded_block(index):
+        return pl.ds(pl.multiple_of(index * (rows + TAIL), rows + TAIL), rows + TAIL)
+
+    own_x = pltpu.make_async_copy(
+        signal_ref.at[:, lanes(me)], x_buf.at[row_block(me)], local_sems.at[0]
+    )
+    own_x.start()
+
+    barrier = pltpu.get_barrier_semaphore()
+    for offset in range(1, count):
+        pl.semaphore_signal(
+            barrier, inc=1, device_id={"ctx": peer_at(offset)}, device_id_type=MESH
+        )
+    pl.semaphore_wait(barrier, count - 1)
+
+    def taps_copy(peer):
+        return pltpu.make_async_remote_copy(
+            src_ref=taps_ref.at[pl.ds(peer * tap_rows, tap_rows)],
+            dst_ref=taps_buf,
+            send_sem=taps_send.at[peer],
+            recv_sem=taps_recv,
+            device_id={"ctx": jnp.int32(peer)},
+            device_id_type=MESH,
+        )
+
+    @pl.when(me == 0)
+    def _():
+        for peer in range(1, count):
+            taps_copy(peer).start()
+        own = pltpu.make_async_copy(taps_ref.at[pl.ds(0, tap_rows)], taps_buf, local_sems.at[1])
+        own.start()
+        own.wait()
+
+    def x_copy(offset):
+        return pltpu.make_async_remote_copy(
+            src_ref=signal_ref.at[:, lanes(peer_at(offset))],
+            dst_ref=x_buf.at[row_block(me)],
+            send_sem=send_x.at[offset],
+            recv_sem=recv_x.at[offset],
+            device_id={"ctx": peer_at(offset)},
+            device_id_type=MESH,
+        )
+
+    def x_arrival(offset):
+        return pltpu.make_async_remote_copy(
+            src_ref=signal_ref.at[:, lanes(peer_at(offset))],
+            dst_ref=x_buf.at[row_block(peer_at(count - offset))],
+            send_sem=send_x.at[offset],
+            recv_sem=recv_x.at[offset],
+            device_id={"ctx": peer_at(offset)},
+            device_id_type=MESH,
+        )
+
+    for offset in range(1, count):
+        x_copy(offset).start()
+
+    @pl.when(me != 0)
+    def _():
+        taps_copy(1).wait_recv()
+
+    row_id = lax.broadcasted_iota(jnp.int32, (rows, rows), 0)
+    col_id = lax.broadcasted_iota(jnp.int32, (rows, rows), 1)
+    flip = (row_id + col_id == rows - 1).astype(jnp.bfloat16)
+    flipped = jnp.dot(taps_buf[...], flip, preferred_element_type=jnp.float32)
+    span = window + rows
+    step = 32
+    for g in range(groups):
+        pieces = [
+            flipped[g * count + d : g * count + d + 1, :] for d in range(count - 1, -1, -1)
+        ]
+        line = jnp.concatenate(pieces + [jnp.zeros((1, rows), jnp.float32)], axis=1)
+        spread = jnp.broadcast_to(line, (step, span))
+        for base in range(0, rows, step):
+            turned = pltpu.roll(
+                spread, (span - (rows - 1) + base) % span, 1, stride=1, stride_axis=0
+            )
+            strip[g, pl.ds(base, step), :] = turned[:, :window].astype(jnp.bfloat16)
+
+    own_x.wait()
+    for offset in range(1, count):
+        x_arrival(offset).wait_recv()
+
+    docs = starts_ref.shape[0]
+    last_start = starts_ref[docs - 1]
+    head_rows = masked_blocks * rows
+    x_head = x_buf[pl.ds(0, head_rows), :]
+    head_id = lax.broadcasted_iota(jnp.int32, (head_rows, width), 0)
+    x_head_masked = jnp.where(
+        head_id >= last_start, x_head.astype(jnp.float32), 0.0
+    ).astype(jnp.bfloat16)
+    lane_group = lax.broadcasted_iota(jnp.int32, (rows, width), 1) // (width // groups)
+
+    for block in range(masked_blocks):
+        depth = (block + 1) * rows
+        t_id = block * rows + lax.broadcasted_iota(jnp.int32, (rows, depth), 0)
+        s_id = lax.broadcasted_iota(jnp.int32, (rows, depth), 1)
+        begin = jnp.zeros((rows, depth), jnp.int32)
+        for k in range(docs):
+            begin = jnp.where(starts_ref[k] <= t_id, jnp.maximum(begin, starts_ref[k]), begin)
+        seen = s_id >= begin
+        total = jnp.zeros((rows, width), jnp.float32)
+        for g in range(groups):
+            taps = jnp.where(
+                seen, strip[g, :, pl.ds(window - depth, depth)].astype(jnp.float32), 0.0
+            ).astype(jnp.bfloat16)
+            part = jnp.dot(taps, x_head[:depth], preferred_element_type=jnp.float32)
+            total = jnp.where(lane_group == g, part, total)
+        store_coded(y_buf, block, total)
+
+    x_buf[pl.ds(0, head_rows), :] = x_head_masked
+    for block in range(masked_blocks, count):
+        depth = (block + 1) * rows
+        total = jnp.zeros((rows, width), jnp.float32)
+        for g in range(groups):
+            part = jnp.dot(
+                strip[g, :, pl.ds(window - depth, depth)],
+                x_buf[pl.ds(0, depth), :],
+                preferred_element_type=jnp.float32,
+            )
+            total = jnp.where(lane_group == g, part, total)
+        store_coded(y_buf, block, total)
+
+    own_y = pltpu.make_async_copy(
+        y_buf.at[coded_block(me)], out_ref.at[:, lanes(me)], local_sems.at[2]
+    )
+    own_y.start()
+
+    def y_copy(offset):
+        return pltpu.make_async_remote_copy(
+            src_ref=y_buf.at[coded_block(peer_at(offset))],
+            dst_ref=out_ref.at[:, lanes(me)],
+            send_sem=send_y.at[offset],
+            recv_sem=recv_y.at[offset],
+            device_id={"ctx": peer_at(offset)},
+            device_id_type=MESH,
+        )
+
+    def y_arrival(offset):
+        return pltpu.make_async_remote_copy(
+            src_ref=y_buf.at[coded_block(peer_at(offset))],
+            dst_ref=out_ref.at[:, lanes(peer_at(count - offset))],
+            send_sem=send_y.at[offset],
+            recv_sem=recv_y.at[offset],
+            device_id={"ctx": peer_at(offset)},
+            device_id_type=MESH,
+        )
+
+    for offset in range(1, count):
+        y_copy(offset).start()
+
+    @pl.when(me == 0)
+    def _():
+        for peer in range(1, count):
+            taps_copy(peer).wait_send()
+
+    for offset in range(1, count):
+        x_copy(offset).wait_send()
+    own_y.wait()
+    for offset in range(1, count):
+        y_arrival(offset).wait_recv()
+    for offset in range(1, count):
+        y_copy(offset).wait_send()
+
+
+def exchanged_body(
+    count, signal, gate_values, skip_gain, filter_base, decay_rate, filter_depth, doc_starts
+):
+    tok_rows, chan_width = signal.shape
+    group_count, lag_width = filter_base.shape
+    window = tok_rows * count
+    ctx_index = lax.axis_index("ctx")
+    lag_index = ctx_index * lag_width + lax.iota(jnp.int32, window)
+    inside = lag_index[None, :] < filter_depth[:, None]
+    panel = jnp.where(
+        inside,
+        filter_base[:, :window].astype(jnp.float32)
+        * jnp.exp(-decay_rate[:, None] * lag_index.astype(jnp.float32)[None, :] / LAGS),
+        0.0,
+    ).astype(jnp.bfloat16)
+    taps = panel.reshape(group_count * count, tok_rows)
+    width = chan_width // count
+    tap_rows = group_count
+    groups = group_count // count
+    masked_blocks = max(1, count // 4)
+    convolved = pl.pallas_call(
+        functools.partial(exchange_kernel, count, masked_blocks),
+        out_shape=jax.ShapeDtypeStruct((tok_rows + TAIL, chan_width), LINK),
+        in_specs=[
+            pl.BlockSpec(memory_space=pl.ANY),
+            pl.BlockSpec(memory_space=pl.ANY),
+            pl.BlockSpec(memory_space=pltpu.SMEM),
+        ],
+        out_specs=pl.BlockSpec(memory_space=pl.ANY),
+        scratch_shapes=[
+            pltpu.VMEM((tap_rows, tok_rows), jnp.bfloat16),
+            pltpu.VMEM((window, width), jnp.bfloat16),
+            pltpu.VMEM((window + count * TAIL, width), LINK),
+            pltpu.VMEM((groups, tok_rows, window), jnp.bfloat16),
+            pltpu.SemaphoreType.DMA((3,)),
+            pltpu.SemaphoreType.DMA((count,)),
+            pltpu.SemaphoreType.DMA,
+            pltpu.SemaphoreType.DMA((count,)),
+            pltpu.SemaphoreType.DMA((count,)),
+            pltpu.SemaphoreType.DMA((count,)),
+            pltpu.SemaphoreType.DMA((count,)),
+        ],
+        compiler_params=pltpu.CompilerParams(
+            collective_id=0, has_side_effects=True, vmem_limit_bytes=32 * 1024 * 1024
+        ),
+    )(signal, taps, doc_starts)
+    unit = jnp.exp2(convolved[tok_rows : tok_rows + 1].astype(jnp.float32)) * (1.0 / TOP)
+    mixed = gate_values.astype(jnp.float32) * (
+        convolved[:tok_rows].astype(jnp.float32) * unit
+        + skip_gain[None, :] * signal.astype(jnp.float32)
+    )
+    return mixed.astype(jnp.bfloat16)
+
+
+def body(signal, gate_values, skip_gain, filter_base, decay_rate, filter_depth, doc_starts, count):
+    tok_rows, chan_width = signal.shape
+    group_count, lag_width = filter_base.shape
+    whole_groups = group_count % count == 0 and chan_width % (count * 128) == 0
+    fits = tok_rows == 256 and lag_width >= tok_rows * count and count % 4 == 0
+    aligned = group_count % 16 == 0
+    arrays = (signal, gate_values, skip_gain, filter_base, decay_rate, filter_depth, doc_starts)
+    if whole_groups and fits and aligned:
+        return exchanged_body(count, *arrays)
+    return gathered_body(*arrays)
+
+
 def solution(mesh):
     in_specs = (
         P("ctx", "chan"),
@@ -94,4 +365,10 @@
         P(),
     )
     out_specs = P("ctx", "chan")
-    return jax.shard_map(body, mesh=mesh, in_specs=in_specs, out_specs=out_specs, check_vma=False)
+    return jax.shard_map(
+        functools.partial(body, count=mesh.shape["ctx"]),
+        mesh=mesh,
+        in_specs=in_specs,
+        out_specs=out_specs,
+        check_vma=False,
+    )

time: 479 us -> 38.9 us (0.08)
  local copies, waits for them, and re-layouts: 358 us -> 3.64 us
  waiting for transfers between devices: 41.7 us -> 0 us
  Pallas kernels: 0 us -> 32.8 us
  blocking collectives: 32.5 us -> 0 us
  matrix products: 18.8 us -> 0 us
  between operations: 13.4 us -> 0.06 us
  loops' own time: 5.29 us -> 0 us
  other arithmetic: 7.3 us -> 2.13 us
    rev x8 -> x0, local copies, waits for them, and re-layouts: 179 us -> none  [toeplitz_apply(): toeplitz = skewed[:, :, :source_rows][:, :, ::-1]]
    reshape x8 -> x1, local copies, waits for them, and re-layouts: 106 us -> 0.04 us  [exchanged_body(): taps = panel.reshape(group_count * count, tok_rows)]
    all_gather x1 -> x0, waiting for transfers between devices: 41 us -> none  [body(): source = lax.all_gather(signal, 'ctx', axis=0, tiled=True)]
    pallas_call x0 -> x1, Pallas kernels: none -> 32.8 us  [exchanged_body(): pl.pallas_call(functools.partial(exchange_kernel, count, masked_blocks),...]
    all_gather x1 -> x0, blocking collectives: 32.5 us -> none  [body(): filters = lax.all_gather(local_panel, 'ctx', axis=1, tiled=True)]
    slice x24 -> x0, local copies, waits for them, and re-layouts: 30.1 us -> none  [the longest x8 17.3 us: toeplitz_apply(): repeated[:, :out_rows * (window_size + 2)]]
    dynamic_slice x24 -> x0, local copies, waits for them, and re-layouts: 19.9 us -> none  [the longest x16 13.4 us: body(): lax.scan(advance, summed, (stacked, jnp.arange(steps_count, dtype=jnp.int...]
    dot_general x8 -> x0, matrix products: 18.8 us -> none  [toeplitz_apply(): jnp.einsum('gts,sgc->tgc', toeplitz, channels, preferred_element_type=jnp...]
  transfers between devices with their start and end apart: 1 -> 0, of which waited for: 1 -> 0; matrix products, arithmetic and copies ran while one was open for 1% -> 0% of each run, Pallas kernels for 0% -> 0%
where the time goes in v1:
time: 38.9 us; the launch traced here: 38.6 us
  Pallas kernels  32.8 us (84%)
  local copies, waits for them, and re-layouts  3.64 us (9%)
  other arithmetic  2.13 us (5%)
    pallas_call x1, Pallas kernels, exchanged_body(): pl.pallas_call(functools.partial(exchange_kernel, count, masked_blocks),...  32.8 us
    unnamed x12, local copies, waits for them, and re-layouts  3.61 us
    convert_element_type x1, other arithmetic, exchanged_body(): return mixed.astype(jnp.bfloat16)  1.16 us
    convert_element_type x1, other arithmetic, exchanged_body(): panel = jnp.where(inside, filter_base[:, :window].astype(jnp.float32) * j...  0.94 us

profile of v1, /device:TPU:26, one launch (start us, length us, event | category | flops | bytes accessed | tf_op | source)
XLA Modules:
  0.0 38.6 jit_solution(7438742611992174581)
XLA Ops:
  0.0 0.0 copy-start.5
  0.0 0.7 %copy-done.5 = f32[16]{0:T(128)S(1)} copy-done((f32[16]{0:T(128)S(1)}, f32[16]{0:T(128)}, u32[]{:S(2)}) %copy-start.5) | copy-done | bytes 88
  0.7 0.0 copy-start.4
  0.7 0.7 %copy-done.4 = s32[16]{0:T(128)S(1)} copy-done((s32[16]{0:T(128)S(1)}, s32[16]{0:T(128)}, u32[]{:S(2)}) %copy-start.4) | copy-done | bytes 88
  1.3 0.9 %select_convert_fusion = bf16[16,2048]{1,0:T(8,128)(2,1)S(1)} fusion(bf16[16,2048]{1,0:T(8,128)(2,1)} %param.10, f32[2048]{0:T(1024)S(1)} %get-tuple-element.6, f32[16]{0:T(128)S(1)} %neg.4, s32[2048]{0:T(1024)S(1)} %get-tuple-element.5, s32[16]{0:T(128)S(1)} %copy-done.4), kind=kLoop, calls=%fused_computation.1 | loop fusion | flops 229376 | bytes 147584 | tf_op jit(solution)/shard_map/convert_element_type | solution.py:305
  2.3 0.0 copy-start.1
  2.3 0.6 %copy-done.1 = s32[5]{0:T(128)S(1)} copy-done((s32[5]{0:T(128)S(1)}, s32[5]{0:T(128)}, u32[]{:S(2)}) %copy-start.1) | copy-done | bytes 44
  2.9 0.0 copy-start
  2.9 1.0 %copy-done = bf16[256,1024]{1,0:T(8,128)(2,1)S(1)} copy-done((bf16[256,1024]{1,0:T(8,128)(2,1)S(1)}, bf16[256,1024]{1,0:T(8,128)(2,1)}, u32[]{:S(2)}) %copy-start) | copy-done | bytes 524312
  4.0 0.0 copy-start.2
  4.0 32.8 %shard_map.73 = s16[272,1024]{1,0:T(8,128)(2,1)S(1)} custom-call(bf16[256,1024]{1,0:T(8,128)(2,1)S(1)} %copy-done, bf16[128,256]{1,0:T(8,128)(2,1)S(1)} %reshape.14.taps_ref, s32[5]{0:T(128)S(1)} %copy-done.1), custom_call_target="tpu_custom_call" | custom-call | tf_op jit(solution)/shard_map/pallas_call | solution.py:311
  36.8 0.0 copy-start.3
  36.8 0.0 copy-done.2
  36.8 0.6 %copy-done.3 = f32[1024]{0:T(1024)S(1)} copy-done((f32[1024]{0:T(1024)S(1)}, f32[1024]{0:T(1024)}, u32[]{:S(2)}) %copy-start.3) | copy-done | bytes 4120
  37.4 1.2 %multiply_convert_fusion = bf16[256,1024]{1,0:T(8,128)(2,1)} fusion(bf16[256,1024]{1,0:T(8,128)(2,1)S(1)} %copy-done, bf16[256,1024]{1,0:T(8,128)(2,1)S(1)} %copy-done.2, f32[1024]{0:T(1024)S(1)} %copy-done.3, f32[1024]{0:T(1024)S(1)} %bitcast.1, s16[272,1024]{1,0:T(8,128)(2,1)S(1)} %shard_map.73), kind=kLoop, calls=%fused_computation | loop fusion | flops 2097152 | bytes 2105344 | tf_op jit(solution)/shard_map/convert_element_type | solution.py:342
  (4 shorter events, 0.1 us)
Async XLA Ops:
  0.0 0.7 %copy-start.5 = (f32[16]{0:T(128)S(1)}, f32[16]{0:T(128)}, u32[]{:S(2)}) copy-start(f32[16]{0:T(128)} %param.11) | copy-start | bytes 196
  0.7 0.7 %copy-start.4 = (s32[16]{0:T(128)S(1)}, s32[16]{0:T(128)}, u32[]{:S(2)}) copy-start(s32[16]{0:T(128)} %param.12) | copy-start | bytes 196
  2.3 0.7 %copy-start.1 = (s32[5]{0:T(128)S(1)}, s32[5]{0:T(128)}, u32[]{:S(2)}) copy-start(s32[5]{0:T(128)} %starts_ref.1) | copy-start | bytes 64
  2.9 1.0 %copy-start = (bf16[256,1024]{1,0:T(8,128)(2,1)S(1)}, bf16[256,1024]{1,0:T(8,128)(2,1)}, u32[]{:S(2)}) copy-start(bf16[256,1024]{1,0:T(8,128)(2,1)} %signal_ref.1) | copy-start | bytes 1572868
  4.0 32.8 %copy-start.2 = (bf16[256,1024]{1,0:T(8,128)(2,1)S(1)}, bf16[256,1024]{1,0:T(8,128)(2,1)}, u32[]{:S(2)}) copy-start(bf16[256,1024]{1,0:T(8,128)(2,1)} %param.8) | copy-start | bytes 1572868
  36.8 0.7 %copy-start.3 = (f32[1024]{0:T(1024)S(1)}, f32[1024]{0:T(1024)}, u32[]{:S(2)}) copy-start(f32[1024]{0:T(1024)} %param.9) | copy-start | bytes 12292

commit v2 on v1

--- a/solution.py
+++ b/solution.py
@@ -90,6 +90,7 @@
 LINK = jnp.int16
 TOP = 32000.0
 TAIL = 16
+VMEM_BYTES = 60 * 1024 * 1024
 MESH = pl.DeviceIdType.MESH
 
 
@@ -105,19 +106,18 @@
 
 
 def exchange_kernel(
-    count, masked_blocks, signal_ref, taps_ref, starts_ref, out_ref,
-    taps_buf, x_buf, y_buf, strip, local_sems, taps_send, taps_recv, send_x, recv_x, send_y, recv_y,
+    count, masked_blocks, signal_ref, base_ref, decay_ref, depth_ref, starts_ref, out_ref,
+    base_buf, taps_all, taps_buf, x_buf, y_buf, strip, decay_mem, depth_mem, starts_mem,
+    local_sems, taps_send, taps_recv, send_x, recv_x, send_y, recv_y,
 ):
     me = lax.axis_index("ctx")
+    half = count // 2
     rows = x_buf.shape[0] // count
     width = x_buf.shape[1]
     tap_rows = taps_buf.shape[0]
     groups = tap_rows // count
     window = rows * count
 
-    def peer_at(offset):
-        return lax.rem(me + offset, count)
-
     def lanes(index):
         return pl.ds(pl.multiple_of(index * width, width), width)
 
@@ -126,22 +126,70 @@
 
     def coded_block(index):
         return pl.ds(pl.multiple_of(index * (rows + TAIL), rows + TAIL), rows + TAIL)
-
-    own_x = pltpu.make_async_copy(
-        signal_ref.at[:, lanes(me)], x_buf.at[row_block(me)], local_sems.at[0]
-    )
-    own_x.start()
 
     barrier = pltpu.get_barrier_semaphore()
     for offset in range(1, count):
         pl.semaphore_signal(
-            barrier, inc=1, device_id={"ctx": peer_at(offset)}, device_id_type=MESH
-        )
+            barrier, inc=1, device_id={"ctx": lax.rem(me + offset, count)}, device_id_type=MESH
+        )
+
+    own_x = pltpu.make_async_copy(
+        signal_ref.at[:, lanes(me)], x_buf.at[row_block(me)], local_sems.at[0]
+    )
+    own_x.start()
+    starts_copy = pltpu.make_async_copy(starts_ref, starts_mem, local_sems.at[1])
+    starts_copy.start()
+    base_copy = pltpu.make_async_copy(base_ref.at[:, pl.ds(0, window)], base_buf, local_sems.at[2])
+    decay_copy = pltpu.make_async_copy(decay_ref, decay_mem, local_sems.at[3])
+    depth_copy = pltpu.make_async_copy(depth_ref, depth_mem, local_sems.at[4])
+
+    @pl.when(me == 0)
+    def _():
+        base_copy.start()
+        decay_copy.start()
+        depth_copy.start()
+
     pl.semaphore_wait(barrier, count - 1)
+
+    def x_copy(peer):
+        return pltpu.make_async_remote_copy(
+            src_ref=signal_ref.at[:, lanes(peer)],
+            dst_ref=x_buf.at[row_block(me)],
+            send_sem=send_x.at[peer],
+            recv_sem=recv_x.at[me],
+            device_id={"ctx": peer},
+            device_id_type=MESH,
+        )
+
+    def x_arrival(source):
+        return pltpu.make_async_remote_copy(
+            src_ref=signal_ref.at[:, lanes(source)],
+            dst_ref=x_buf.at[row_block(source)],
+            send_sem=send_x.at[source],
+            recv_sem=recv_x.at[source],
+            device_id={"ctx": jnp.int32(source)},
+            device_id_type=MESH,
+        )
+
+    side = lax.div(me, half)
+    place = lax.rem(me, half)
+    near = [side * half + lax.rem(place + k, half) for k in range(1, half)]
+    far = [(1 - side) * half + lax.rem(place + k, half) for k in range(half)]
+    early = place < half // 2
+
+    @pl.when(early)
+    def _():
+        for peer in far + near:
+            x_copy(peer).start()
+
+    @pl.when(jnp.logical_not(early))
+    def _():
+        for peer in near + far:
+            x_copy(peer).start()
 
     def taps_copy(peer):
         return pltpu.make_async_remote_copy(
-            src_ref=taps_ref.at[pl.ds(peer * tap_rows, tap_rows)],
+            src_ref=taps_all.at[pl.ds(peer * tap_rows, tap_rows)],
             dst_ref=taps_buf,
             send_sem=taps_send.at[peer],
             recv_sem=taps_recv,
@@ -151,34 +199,32 @@
 
     @pl.when(me == 0)
     def _():
+        base_copy.wait()
+        decay_copy.wait()
+        depth_copy.wait()
+        group_rows = groups * count
+        group_id = lax.broadcasted_iota(jnp.int32, (group_rows, 128), 0)
+        decay = jnp.zeros((group_rows, 128), jnp.float32)
+        depth = jnp.zeros((group_rows, 128), jnp.int32)
+        for g in range(group_rows):
+            decay = jnp.where(group_id == g, decay_mem[g], decay)
+            depth = jnp.where(group_id == g, depth_mem[g], depth)
+        decay = jnp.concatenate([decay] * (rows // 128), axis=1)
+        depth = jnp.concatenate([depth] * (rows // 128), axis=1)
+        out_row = lax.broadcasted_iota(jnp.int32, (group_rows * count, group_rows), 0)
+        in_row = lax.broadcasted_iota(jnp.int32, (group_rows * count, group_rows), 1)
+        placed = jnp.zeros((group_rows * count, rows), jnp.float32)
+        for d in range(count):
+            lag = d * rows + lax.broadcasted_iota(jnp.int32, (group_rows, rows), 1)
+            base = base_buf[:, pl.ds(d * rows, rows)].astype(jnp.float32)
+            kept = base * jnp.exp(-decay * lag.astype(jnp.float32) / LAGS)
+            panel = jnp.where(lag < depth, kept, 0.0).astype(jnp.bfloat16)
+            pick = (out_row == in_row * count + d).astype(jnp.float32).astype(jnp.bfloat16)
+            placed += jnp.dot(pick, panel, preferred_element_type=jnp.float32)
+        taps_all[...] = placed.astype(jnp.bfloat16)
         for peer in range(1, count):
             taps_copy(peer).start()
-        own = pltpu.make_async_copy(taps_ref.at[pl.ds(0, tap_rows)], taps_buf, local_sems.at[1])
-        own.start()
-        own.wait()
-
-    def x_copy(offset):
-        return pltpu.make_async_remote_copy(
-            src_ref=signal_ref.at[:, lanes(peer_at(offset))],
-            dst_ref=x_buf.at[row_block(me)],
-            send_sem=send_x.at[offset],
-            recv_sem=recv_x.at[offset],
-            device_id={"ctx": peer_at(offset)},
-            device_id_type=MESH,
-        )
-
-    def x_arrival(offset):
-        return pltpu.make_async_remote_copy(
-            src_ref=signal_ref.at[:, lanes(peer_at(offset))],
-            dst_ref=x_buf.at[row_block(peer_at(count - offset))],
-            send_sem=send_x.at[offset],
-            recv_sem=recv_x.at[offset],
-            device_id={"ctx": peer_at(offset)},
-            device_id_type=MESH,
-        )
-
-    for offset in range(1, count):
-        x_copy(offset).start()
+        taps_buf[...] = taps_all[pl.ds(0, tap_rows), :]
 
     @pl.when(me != 0)
     def _():
@@ -186,7 +232,7 @@
 
     row_id = lax.broadcasted_iota(jnp.int32, (rows, rows), 0)
     col_id = lax.broadcasted_iota(jnp.int32, (rows, rows), 1)
-    flip = (row_id + col_id == rows - 1).astype(jnp.bfloat16)
+    flip = (row_id + col_id == rows - 1).astype(jnp.float32).astype(jnp.bfloat16)
     flipped = jnp.dot(taps_buf[...], flip, preferred_element_type=jnp.float32)
     span = window + rows
     step = 32
@@ -202,39 +248,78 @@
             )
             strip[g, pl.ds(base, step), :] = turned[:, :window].astype(jnp.bfloat16)
 
+    starts_copy.wait()
     own_x.wait()
-    for offset in range(1, count):
-        x_arrival(offset).wait_recv()
-
-    docs = starts_ref.shape[0]
-    last_start = starts_ref[docs - 1]
+    docs = starts_mem.shape[0]
     head_rows = masked_blocks * rows
-    x_head = x_buf[pl.ds(0, head_rows), :]
-    head_id = lax.broadcasted_iota(jnp.int32, (head_rows, width), 0)
-    x_head_masked = jnp.where(
-        head_id >= last_start, x_head.astype(jnp.float32), 0.0
-    ).astype(jnp.bfloat16)
     lane_group = lax.broadcasted_iota(jnp.int32, (rows, width), 1) // (width // groups)
 
+    def wait_for(block):
+        @pl.when(me != block)
+        def _():
+            x_arrival(block).wait_recv()
+
+    def y_copy(block):
+        return pltpu.make_async_remote_copy(
+            src_ref=y_buf.at[coded_block(block)],
+            dst_ref=out_ref.at[:, lanes(me)],
+            send_sem=send_y.at[block],
+            recv_sem=recv_y.at[me],
+            device_id={"ctx": jnp.int32(block)},
+            device_id_type=MESH,
+        )
+
+    def y_arrival(source):
+        return pltpu.make_async_remote_copy(
+            src_ref=y_buf.at[coded_block(source)],
+            dst_ref=out_ref.at[:, lanes(source)],
+            send_sem=send_y.at[source],
+            recv_sem=recv_y.at[source],
+            device_id={"ctx": jnp.int32(source)},
+            device_id_type=MESH,
+        )
+
+    own_y = pltpu.make_async_copy(
+        y_buf.at[coded_block(me)], out_ref.at[:, lanes(me)], local_sems.at[5]
+    )
+
+    def send_back(block, total):
+        store_coded(y_buf, block, total)
+
+        @pl.when(me != block)
+        def _():
+            y_copy(block).start()
+
+        @pl.when(me == block)
+        def _():
+            own_y.start()
+
     for block in range(masked_blocks):
+        wait_for(block)
         depth = (block + 1) * rows
         t_id = block * rows + lax.broadcasted_iota(jnp.int32, (rows, depth), 0)
         s_id = lax.broadcasted_iota(jnp.int32, (rows, depth), 1)
         begin = jnp.zeros((rows, depth), jnp.int32)
         for k in range(docs):
-            begin = jnp.where(starts_ref[k] <= t_id, jnp.maximum(begin, starts_ref[k]), begin)
+            start = starts_mem[k]
+            begin = jnp.where(start <= t_id, jnp.maximum(begin, start), begin)
         seen = s_id >= begin
         total = jnp.zeros((rows, width), jnp.float32)
         for g in range(groups):
             taps = jnp.where(
                 seen, strip[g, :, pl.ds(window - depth, depth)].astype(jnp.float32), 0.0
             ).astype(jnp.bfloat16)
-            part = jnp.dot(taps, x_head[:depth], preferred_element_type=jnp.float32)
+            part = jnp.dot(taps, x_buf[pl.ds(0, depth), :], preferred_element_type=jnp.float32)
             total = jnp.where(lane_group == g, part, total)
-        store_coded(y_buf, block, total)
-
-    x_buf[pl.ds(0, head_rows), :] = x_head_masked
+        send_back(block, total)
+
+    head_id = lax.broadcasted_iota(jnp.int32, (head_rows, width), 0)
+    x_head = x_buf[pl.ds(0, head_rows), :].astype(jnp.float32)
+    x_buf[pl.ds(0, head_rows), :] = jnp.where(
+        head_id >= starts_mem[docs - 1], x_head, 0.0
+    ).astype(jnp.bfloat16)
     for block in range(masked_blocks, count):
+        wait_for(block)
         depth = (block + 1) * rows
         total = jnp.zeros((rows, width), jnp.float32)
         for g in range(groups):
@@ -244,48 +329,20 @@
                 preferred_element_type=jnp.float32,
             )
             total = jnp.where(lane_group == g, part, total)
-        store_coded(y_buf, block, total)
-
-    own_y = pltpu.make_async_copy(
-        y_buf.at[coded_block(me)], out_ref.at[:, lanes(me)], local_sems.at[2]
-    )
-    own_y.start()
-
-    def y_copy(offset):
-        return pltpu.make_async_remote_copy(
-            src_ref=y_buf.at[coded_block(peer_at(offset))],
-            dst_ref=out_ref.at[:, lanes(me)],
-            send_sem=send_y.at[offset],
-            recv_sem=recv_y.at[offset],
-            device_id={"ctx": peer_at(offset)},
-            device_id_type=MESH,
-        )
-
-    def y_arrival(offset):
-        return pltpu.make_async_remote_copy(
-            src_ref=y_buf.at[coded_block(peer_at(offset))],
-            dst_ref=out_ref.at[:, lanes(peer_at(count - offset))],
-            send_sem=send_y.at[offset],
-            recv_sem=recv_y.at[offset],
-            device_id={"ctx": peer_at(offset)},
-            device_id_type=MESH,
-        )
-
-    for offset in range(1, count):
-        y_copy(offset).start()
+        send_back(block, total)
 
     @pl.when(me == 0)
     def _():
         for peer in range(1, count):
             taps_copy(peer).wait_send()
 
-    for offset in range(1, count):
-        x_copy(offset).wait_send()
+    for peer in near + far:
+        x_copy(peer).wait_send()
     own_y.wait()
-    for offset in range(1, count):
-        y_arrival(offset).wait_recv()
-    for offset in range(1, count):
-        y_copy(offset).wait_send()
+    for peer in near + far:
+        y_arrival(peer).wait_recv()
+    for peer in near + far:
+        y_arrival(peer).wait_send()
 
 
 def exchanged_body(
@@ -294,16 +351,6 @@
     tok_rows, chan_width = signal.shape
     group_count, lag_width = filter_base.shape
     window = tok_rows * count
-    ctx_index = lax.axis_index("ctx")
-    lag_index = ctx_index * lag_width + lax.iota(jnp.int32, window)
-    inside = lag_index[None, :] < filter_depth[:, None]
-    panel = jnp.where(
-        inside,
-        filter_base[:, :window].astype(jnp.float32)
-        * jnp.exp(-decay_rate[:, None] * lag_index.astype(jnp.float32)[None, :] / LAGS),
-        0.0,
-    ).astype(jnp.bfloat16)
-    taps = panel.reshape(group_count * count, tok_rows)
     width = chan_width // count
     tap_rows = group_count
     groups = group_count // count
@@ -313,16 +360,20 @@
         out_shape=jax.ShapeDtypeStruct((tok_rows + TAIL, chan_width), LINK),
         in_specs=[
             pl.BlockSpec(memory_space=pl.ANY),
-            pl.BlockSpec(memory_space=pl.ANY),
-            pl.BlockSpec(memory_space=pltpu.SMEM),
-        ],
+        ]
+        * 5,
         out_specs=pl.BlockSpec(memory_space=pl.ANY),
         scratch_shapes=[
+            pltpu.VMEM((group_count, window), jnp.bfloat16),
+            pltpu.VMEM((tap_rows * count, tok_rows), jnp.bfloat16),
             pltpu.VMEM((tap_rows, tok_rows), jnp.bfloat16),
             pltpu.VMEM((window, width), jnp.bfloat16),
             pltpu.VMEM((window + count * TAIL, width), LINK),
             pltpu.VMEM((groups, tok_rows, window), jnp.bfloat16),
-            pltpu.SemaphoreType.DMA((3,)),
+            pltpu.SMEM(decay_rate.shape, jnp.float32),
+            pltpu.SMEM(filter_depth.shape, jnp.int32),
+            pltpu.SMEM(doc_starts.shape, jnp.int32),
+            pltpu.SemaphoreType.DMA((6,)),
             pltpu.SemaphoreType.DMA((count,)),
             pltpu.SemaphoreType.DMA,
             pltpu.SemaphoreType.DMA((count,)),
@@ -331,9 +382,9 @@
             pltpu.SemaphoreType.DMA((count,)),
         ],
         compiler_params=pltpu.CompilerParams(
-            collective_id=0, has_side_effects=True, vmem_limit_bytes=32 * 1024 * 1024
+            collective_id=0, has_side_effects=True, vmem_limit_bytes=VMEM_BYTES
         ),
-    )(signal, taps, doc_starts)
+    )(signal, filter_base, decay_rate, filter_depth, doc_starts)
     unit = jnp.exp2(convolved[tok_rows : tok_rows + 1].astype(jnp.float32)) * (1.0 / TOP)
     mixed = gate_values.astype(jnp.float32) * (
         convolved[:tok_rows].astype(jnp.float32) * unit

time: 38.9 us -> 32.7 us (0.84)
  local copies, waits for them, and re-layouts: 3.64 us -> 0.01 us
  Pallas kernels: 32.8 us -> 29.4 us
  other arithmetic: 2.13 us -> 2.94 us
    unnamed x12 -> x6, local copies, waits for them, and re-layouts: 3.61 us -> 0.01 us
    pallas_call x1, Pallas kernels: 32.8 us -> 29.4 us  [exchanged_body(): pl.pallas_call(functools.partial(exchange_kernel, count, masked_blocks),...]
    convert_element_type x1, other arithmetic: 1.16 us -> 2.2 us  [exchanged_body(): return mixed.astype(jnp.bfloat16)]
    convert_element_type x1 -> x0, other arithmetic: 0.94 us -> none  [exchanged_body(): panel = jnp.where(inside, filter_base[:, :window].astype(jnp.float32) * j...]
    mul x1, other arithmetic: 0.02 us -> 0.74 us  [exchanged_body(): jnp.exp2(convolved[tok_rows:tok_rows + 1].astype(jnp.float32)) * (1.0 / TOP)]
where the time goes in v2:
time: 32.7 us; the launch traced here: 32.4 us
  Pallas kernels  29.4 us (90%)
  other arithmetic  2.94 us (9%)
    pallas_call x1, Pallas kernels, exchanged_body(): pl.pallas_call(functools.partial(exchange_kernel, count, masked_blocks),...  29.4 us
    convert_element_type x1, other arithmetic, exchanged_body(): return mixed.astype(jnp.bfloat16)  2.2 us
    mul x1, other arithmetic, exchanged_body(): jnp.exp2(convolved[tok_rows:tok_rows + 1].astype(jnp.float32)) * (1.0 / TOP)  0.74 us

profile of v2, /device:TPU:26, one launch (start us, length us, event | category | flops | bytes accessed | tf_op | source)
XLA Modules:
  0.0 32.4 jit_solution(2153935635567547966)
XLA Ops:
  0.0 0.0 copy-start
  0.0 0.0 copy-start.1
  0.0 29.4 %shard_map.73 = s16[272,1024]{1,0:T(8,128)(2,1)} custom-call(bf16[256,1024]{1,0:T(8,128)(2,1)} %signal_ref.1, bf16[16,2048]{1,0:T(8,128)(2,1)} %base_ref.1, f32[16]{0:T(128)} %decay_ref.1, s32[16]{0:T(128)} %depth_ref.1, s32[5]{0:T(128)} %starts_ref.1), custom_call_target="tpu_custom_call" | custom-call | tf_op jit(solution)/shard_map/pallas_call | solution.py:358
  29.4 0.0 copy-start.2
  29.5 0.7 %exponential_multiply_fusion = f32[1,1024]{1,0:T(1,128)S(1)} fusion(s16[272,1024]{1,0:T(8,128)(2,1)} %shard_map.73), kind=kLoop, calls=%fused_computation.1 | loop fusion | flops 3072 | bytes 6144 | tf_op jit(solution)/shard_map/mul | solution.py:388
  30.2 0.0 copy-done
  30.2 0.0 copy-done.1
  30.2 0.0 copy-done.2
  30.2 2.2 %multiply_convert_fusion = bf16[256,1024]{1,0:T(8,128)(2,1)} fusion(bf16[256,1024]{1,0:T(8,128)(2,1)S(1)} %copy-done, bf16[256,1024]{1,0:T(8,128)(2,1)S(1)} %copy-done.1, f32[1024]{0:T(1024)S(1)} %copy-done.2, f32[1024]{0:T(1024)S(1)} %bitcast.1, s16[272,1024]{1,0:T(8,128)(2,1)} %shard_map.73), kind=kLoop, calls=%fused_computation | loop fusion | flops 2097152 | bytes 2105344 | tf_op jit(solution)/shard_map/convert_element_type | solution.py:393
Async XLA Ops:
  0.0 30.2 %copy-start = (bf16[256,1024]{1,0:T(8,128)(2,1)S(1)}, bf16[256,1024]{1,0:T(8,128)(2,1)}, u32[]{:S(2)}) copy-start(bf16[256,1024]{1,0:T(8,128)(2,1)} %signal_ref.1) | copy-start | bytes 1572868
  0.0 30.2 %copy-start.1 = (bf16[256,1024]{1,0:T(8,128)(2,1)S(1)}, bf16[256,1024]{1,0:T(8,128)(2,1)}, u32[]{:S(2)}) copy-start(bf16[256,1024]{1,0:T(8,128)(2,1)} %param.8) | copy-start | bytes 1572868
  29.4 0.8 %copy-start.2 = (f32[1024]{0:T(1024)S(1)}, f32[1024]{0:T(1024)}, u32[]{:S(2)}) copy-start(f32[1024]{0:T(1024)} %param.9) | copy-start | bytes 12292

commit v3 on v2

--- a/solution.py
+++ b/solution.py
@@ -88,27 +88,28 @@
 
 
 LINK = jnp.int16
-TOP = 32000.0
-TAIL = 16
+STEPS = 780.0
+FLOOR = 30.0
 VMEM_BYTES = 60 * 1024 * 1024
 MESH = pl.DeviceIdType.MESH
 
 
-def store_coded(y_buf, block, total):
-    rows, width = total.shape
-    peak = jnp.maximum(jnp.max(jnp.abs(total), axis=0, keepdims=True), 1e-30)
-    exponent = jnp.ceil(jnp.log2(peak))
-    coded = jnp.floor(total * (jnp.exp2(-exponent) * TOP) + 0.5)
-    first = block * (rows + TAIL)
-    y_buf[pl.ds(first, rows), :] = coded.astype(jnp.int32).astype(LINK)
-    tail = jnp.broadcast_to(exponent, (TAIL, width))
-    y_buf[pl.ds(first + rows, TAIL), :] = tail.astype(jnp.int32).astype(LINK)
+def coded(values):
+    size = jnp.maximum(jnp.abs(values), 2.0**-FLOOR)
+    steps = jnp.floor((jnp.log2(size) + FLOOR) * STEPS + 0.5)
+    return jnp.where(values < 0.0, -steps, steps).astype(jnp.int32).astype(LINK)
+
+
+def decoded(codes):
+    steps = codes.astype(jnp.int32).astype(jnp.float32)
+    size = jnp.exp2(jnp.abs(steps) * (1.0 / STEPS) - FLOOR)
+    return jnp.where(steps == 0.0, 0.0, jnp.where(steps < 0.0, -size, size))
 
 
 def exchange_kernel(
-    count, masked_blocks, signal_ref, base_ref, decay_ref, depth_ref, starts_ref, out_ref,
-    base_buf, taps_all, taps_buf, x_buf, y_buf, strip, decay_mem, depth_mem, starts_mem,
-    local_sems, taps_send, taps_recv, send_x, recv_x, send_y, recv_y,
+    count, masked_blocks, signal_ref, gate_ref, skip_ref, base_ref, decay_ref, depth_ref,
+    starts_ref, out_ref, base_buf, taps_all, taps_buf, x_buf, y_buf, y_in, own_signal, gate_buf,
+    skip_buf, mixed_buf, strip, decay_mem, depth_mem, starts_mem, local_sems, out_sems, taps_send, taps_recv, send_x, recv_x, send_y, recv_y,
 ):
     me = lax.axis_index("ctx")
     half = count // 2
@@ -124,9 +125,6 @@
     def row_block(index):
         return pl.ds(pl.multiple_of(index * rows, rows), rows)
 
-    def coded_block(index):
-        return pl.ds(pl.multiple_of(index * (rows + TAIL), rows + TAIL), rows + TAIL)
-
     barrier = pltpu.get_barrier_semaphore()
     for offset in range(1, count):
         pl.semaphore_signal(
@@ -149,6 +147,11 @@
         decay_copy.start()
         depth_copy.start()
 
+    operand_copies = [
+        pltpu.make_async_copy(signal_ref, own_signal, local_sems.at[5]),
+        pltpu.make_async_copy(gate_ref, gate_buf, local_sems.at[6]),
+        pltpu.make_async_copy(skip_ref, skip_buf, local_sems.at[7]),
+    ]
     pl.semaphore_wait(barrier, count - 1)
 
     def x_copy(peer):
@@ -226,6 +229,9 @@
             taps_copy(peer).start()
         taps_buf[...] = taps_all[pl.ds(0, tap_rows), :]
 
+    for copy in operand_copies:
+        copy.start()
+
     @pl.when(me != 0)
     def _():
         taps_copy(1).wait_recv()
@@ -261,8 +267,8 @@
 
     def y_copy(block):
         return pltpu.make_async_remote_copy(
-            src_ref=y_buf.at[coded_block(block)],
-            dst_ref=out_ref.at[:, lanes(me)],
+            src_ref=y_buf.at[row_block(block)],
+            dst_ref=y_in.at[row_block(me)],
             send_sem=send_y.at[block],
             recv_sem=recv_y.at[me],
             device_id={"ctx": jnp.int32(block)},
@@ -271,28 +277,20 @@
 
     def y_arrival(source):
         return pltpu.make_async_remote_copy(
-            src_ref=y_buf.at[coded_block(source)],
-            dst_ref=out_ref.at[:, lanes(source)],
+            src_ref=y_buf.at[row_block(source)],
+            dst_ref=y_in.at[row_block(source)],
             send_sem=send_y.at[source],
             recv_sem=recv_y.at[source],
             device_id={"ctx": jnp.int32(source)},
             device_id_type=MESH,
         )
 
-    own_y = pltpu.make_async_copy(
-        y_buf.at[coded_block(me)], out_ref.at[:, lanes(me)], local_sems.at[5]
-    )
-
     def send_back(block, total):
-        store_coded(y_buf, block, total)
+        y_buf[pl.ds(block * rows, rows), :] = coded(total)
 
         @pl.when(me != block)
         def _():
             y_copy(block).start()
-
-        @pl.when(me == block)
-        def _():
-            own_y.start()
 
     for block in range(masked_blocks):
         wait_for(block)
@@ -331,6 +329,25 @@
             total = jnp.where(lane_group == g, part, total)
         send_back(block, total)
 
+    for copy in operand_copies:
+        copy.wait()
+
+    def out_copy(index):
+        return pltpu.make_async_copy(
+            mixed_buf.at[:, lanes(index)], out_ref.at[:, lanes(index)], out_sems.at[index]
+        )
+
+    def mix(index, codes):
+        direct = skip_buf[:, lanes(index)] * own_signal[:, lanes(index)].astype(jnp.float32)
+        gates = gate_buf[:, lanes(index)].astype(jnp.float32)
+        mixed_buf[:, lanes(index)] = (gates * (decoded(codes) + direct)).astype(jnp.bfloat16)
+        out_copy(index).start()
+
+    mix(me, y_buf[row_block(me), :])
+    for peer in near + far:
+        y_arrival(peer).wait_recv()
+        mix(peer, y_in[row_block(peer), :])
+
     @pl.when(me == 0)
     def _():
         for peer in range(1, count):
@@ -338,11 +355,10 @@
 
     for peer in near + far:
         x_copy(peer).wait_send()
-    own_y.wait()
-    for peer in near + far:
-        y_arrival(peer).wait_recv()
     for peer in near + far:
         y_arrival(peer).wait_send()
+    for index in range(count):
+        out_copy(index).wait()
 
 
 def exchanged_body(
@@ -355,25 +371,31 @@
     tap_rows = group_count
     groups = group_count // count
     masked_blocks = max(1, count // 4)
-    convolved = pl.pallas_call(
+    return pl.pallas_call(
         functools.partial(exchange_kernel, count, masked_blocks),
-        out_shape=jax.ShapeDtypeStruct((tok_rows + TAIL, chan_width), LINK),
+        out_shape=jax.ShapeDtypeStruct((tok_rows, chan_width), jnp.bfloat16),
         in_specs=[
             pl.BlockSpec(memory_space=pl.ANY),
         ]
-        * 5,
+        * 7,
         out_specs=pl.BlockSpec(memory_space=pl.ANY),
         scratch_shapes=[
             pltpu.VMEM((group_count, window), jnp.bfloat16),
             pltpu.VMEM((tap_rows * count, tok_rows), jnp.bfloat16),
             pltpu.VMEM((tap_rows, tok_rows), jnp.bfloat16),
             pltpu.VMEM((window, width), jnp.bfloat16),
-            pltpu.VMEM((window + count * TAIL, width), LINK),
+            pltpu.VMEM((window, width), LINK),
+            pltpu.VMEM((window, width), LINK),
+            pltpu.VMEM((tok_rows, chan_width), jnp.bfloat16),
+            pltpu.VMEM((tok_rows, chan_width), jnp.bfloat16),
+            pltpu.VMEM((1, chan_width), jnp.float32),
+            pltpu.VMEM((tok_rows, chan_width), jnp.bfloat16),
             pltpu.VMEM((groups, tok_rows, window), jnp.bfloat16),
             pltpu.SMEM(decay_rate.shape, jnp.float32),
             pltpu.SMEM(filter_depth.shape, jnp.int32),
             pltpu.SMEM(doc_starts.shape, jnp.int32),
-            pltpu.SemaphoreType.DMA((6,)),
+            pltpu.SemaphoreType.DMA((8,)),
+            pltpu.SemaphoreType.DMA((count,)),
             pltpu.SemaphoreType.DMA((count,)),
             pltpu.SemaphoreType.DMA,
             pltpu.SemaphoreType.DMA((count,)),
@@ -384,13 +406,15 @@
         compiler_params=pltpu.CompilerParams(
             collective_id=0, has_side_effects=True, vmem_limit_bytes=VMEM_BYTES
         ),
-    )(signal, filter_base, decay_rate, filter_depth, doc_starts)
-    unit = jnp.exp2(convolved[tok_rows : tok_rows + 1].astype(jnp.float32)) * (1.0 / TOP)
-    mixed = gate_values.astype(jnp.float32) * (
-        convolved[:tok_rows].astype(jnp.float32) * unit
-        + skip_gain[None, :] * signal.astype(jnp.float32)
-    )
-    return mixed.astype(jnp.bfloat16)
+    )(
+        signal,
+        gate_values,
+        skip_gain.reshape(1, chan_width),
+        filter_base,
+        decay_rate,
+        filter_depth,
+        doc_starts,
+    )
 
 
 def body(signal, gate_values, skip_gain, filter_base, decay_rate, filter_depth, doc_starts, count):

time: 32.7 us -> 31.8 us (0.972)
  the two profiles are of different devices: /device:TPU:26 before, /device:TPU:0 now
where the time goes in v3:
time: 31.8 us; the launch traced here: 31.6 us
  Pallas kernels  29.8 us (94%)
  local copies, waits for them, and re-layouts  1.87 us (6%)
    pallas_call x1, Pallas kernels, exchanged_body(): pl.pallas_call(functools.partial(exchange_kernel, count, masked_blocks),...  29.8 us
    unnamed x1, local copies, waits for them, and re-layouts  1.87 us

profile of v3, /device:TPU:0, one launch (start us, length us, event | category | flops | bytes accessed | tf_op | source)
XLA Modules:
  0.0 31.6 jit_solution(4770007475603644181)
XLA Ops:
  0.0 29.8 %shard_map.73 = bf16[256,1024]{1,0:T(8,128)(2,1)} custom-call(bf16[256,1024]{1,0:T(8,128)(2,1)} %signal_ref.1, bf16[256,1024]{1,0:T(8,128)(2,1)} %gate_ref.1, f32[1,1024]{1,0:T(1,128)} %bitcast.1, bf16[16,2048]{1,0:T(8,128)(2,1)} %base_ref.1, f32[16]{0:T(128)} %decay_ref.1, s32[16]{0:T(128)} %depth_ref.1, s32[5]{0:T(128)} %starts_ref.1), custom_call_target="tpu_custom_call" | custom-call | tf_op jit(solution)/shard_map/pallas_call | solution.py:374
  29.8 1.9 %copy.9 = bf16[256,1024]{1,0:T(8,128)(2,1)} copy(bf16[256,1024]{1,0:T(8,128)(2,1)} %shard_map.73) | data formatting | bytes 1048576

commit v4 on v3

--- a/solution.py
+++ b/solution.py
@@ -373,7 +373,7 @@
     masked_blocks = max(1, count // 4)
     return pl.pallas_call(
         functools.partial(exchange_kernel, count, masked_blocks),
-        out_shape=jax.ShapeDtypeStruct((tok_rows, chan_width), jnp.bfloat16),
+        out_shape=pltpu.VMEM((tok_rows, chan_width), jnp.bfloat16),
         in_specs=[
             pl.BlockSpec(memory_space=pl.ANY),
         ]

time: 31.8 us -> 30.3 us (0.953)
  local copies, waits for them, and re-layouts: 1.87 us -> 0.8 us
  Pallas kernels: 29.8 us -> 29.3 us
    unnamed x1, local copies, waits for them, and re-layouts: 1.87 us -> 0.8 us
    pallas_call x1, Pallas kernels: 29.8 us -> 29.3 us  [exchanged_body(): pl.pallas_call(functools.partial(exchange_kernel, count, masked_blocks),...]
where the time goes in v4:
time: 30.3 us; the launch traced here: 30.1 us
  Pallas kernels  29.3 us (97%)
  local copies, waits for them, and re-layouts  0.8 us (3%)
    pallas_call x1, Pallas kernels, exchanged_body(): pl.pallas_call(functools.partial(exchange_kernel, count, masked_blocks),...  29.3 us
    unnamed x1, local copies, waits for them, and re-layouts  0.8 us

profile of v4, /device:TPU:0, one launch (start us, length us, event | category | flops | bytes accessed | tf_op | source)
XLA Modules:
  0.0 30.1 jit_solution(11834657839129401165)
XLA Ops:
  0.0 29.3 %shard_map.73 = bf16[256,1024]{1,0:T(8,128)(2,1)S(1)} custom-call(bf16[256,1024]{1,0:T(8,128)(2,1)} %signal_ref.1, bf16[256,1024]{1,0:T(8,128)(2,1)} %gate_ref.1, f32[1,1024]{1,0:T(1,128)} %bitcast.1, bf16[16,2048]{1,0:T(8,128)(2,1)} %base_ref.1, f32[16]{0:T(128)} %decay_ref.1, s32[16]{0:T(128)} %depth_ref.1, s32[5]{0:T(128)} %starts_ref.1), custom_call_target="tpu_custom_call" | custom-call | tf_op jit(solution)/shard_map/pallas_call | solution.py:374
  29.3 0.8 %copy.9 = bf16[256,1024]{1,0:T(8,128)(2,1)} copy(bf16[256,1024]{1,0:T(8,128)(2,1)S(1)} %shard_map.73) | data formatting | bytes 1048576
